TPU v7x, 512 devices: a whole 4x8x8 slice. The times are simulated.
512 devices in a mesh: row: 4 (over x), col: 64 (over z, y), leaf: 2 (over core).
Axes of the slice: x: 4, y: 8, z: 8, core: 2. Of those that a mesh axis runs over, the one named last changes fastest.
Arguments:
- bottom_rhs: bfloat16 [512, 256, 128], P(('row', 'col', 'leaf')), may hold values from -6 to 6
- top_rhs: bfloat16 [8, 256, 128], P('row'), may hold values from -6 to 6
- bottom_linv: bfloat16 [512, 256, 256], P(('row', 'col', 'leaf')), may hold values from -2 to 2
- bottom_uinv: bfloat16 [512, 256, 256], P(('row', 'col', 'leaf')), may hold values from -2 to 2
- top_linv: bfloat16 [8, 256, 256], P('row'), may hold values from -2 to 2
- top_uinv: bfloat16 [8, 256, 256], P('row'), may hold values from -2 to 2
- lower_blocks: bfloat16 [8, 64, 2, 4, 256, 256], P('row', 'col', 'leaf'), may hold values from -0.0234375 to 0.0234375
- upper_blocks: bfloat16 [8, 64, 2, 4, 256, 256], P('row', 'col', 'leaf'), may hold values from -0.1875 to 0.1875
- bottom_width: int32 [512], P(('row', 'col', 'leaf')), may hold values from 128 to 256
- top_width: int32 [8], P('row'), may hold values from 128 to 256
- pattern: int32 [8, 64, 2, 4], P('row', 'col', 'leaf'), may hold values 0 or 1
- parent: int32 [64, 2, 4], P('col', 'leaf'), may hold values from 0 to 7
Outputs:
- bottom_solution: float32 [512, 256, 128], P(('row', 'col', 'leaf'))
- top_solution: float32 [8, 256, 128], P('row')
All inputs are finite; a program needn't handle non-finite values. No bound on the sum of `pattern` on one device may be relied on, other than what follows from the above.
Results may differ from a plain program's by a relative error of at most 0.0056.
Values may be sent and summed in bfloat16 or wider, within the bound.
A program may use at most 64 MiB of HBM per device.

v0:
```python
import jax
import jax.numpy as jnp
from jax import lax
from jax.sharding import PartitionSpec as P

W = 256
TPR = 2


def apply_blocks(blocks, vectors):
    return jnp.einsum("bvw,bwn->bvn", blocks, vectors, preferred_element_type=jnp.float32)


def solve_top(top_rhs, merged, top_linv, top_uinv, top_mask):
    top_diff = ((top_rhs.astype(jnp.float32) - merged) * top_mask[..., None]).astype(jnp.bfloat16)
    top_y = (apply_blocks(top_linv, top_diff) * top_mask[..., None]).astype(jnp.bfloat16)
    return apply_blocks(top_uinv, top_y) * top_mask[..., None]


def local(
    bottom_rhs,
    top_rhs,
    bottom_linv,
    bottom_uinv,
    top_linv,
    top_uinv,
    lower_blocks,
    upper_blocks,
    bottom_width,
    top_width,
    pattern,
    parent,
):
    places = jnp.arange(W, dtype=jnp.int32)
    bottom_mask = (places[None, :] < bottom_width[:, None]).astype(jnp.float32)
    top_mask = (places[None, :] < top_width[:, None]).astype(jnp.float32)
    tops = lax.axis_index("row") * TPR + jnp.arange(TPR, dtype=jnp.int32)
    couple = ((pattern[:, 0, 0, :] > 0) | (parent[0, 0][None, :] == tops[:, None])).astype(
        jnp.bfloat16
    )
    masked_rhs = bottom_rhs * bottom_mask.astype(jnp.bfloat16)[..., None]
    bottom_y = (apply_blocks(bottom_linv, masked_rhs) * bottom_mask[..., None]).astype(jnp.bfloat16)
    column_values = lax.all_gather(bottom_y, "row", axis=0, tiled=True)
    lower_local = lower_blocks[:, 0, 0] * couple[:, :, None, None]
    partial_value = jnp.einsum(
        "kjvw,jwn->kvn", lower_local, column_values, preferred_element_type=jnp.float32
    )
    merged = lax.psum(partial_value, ("col", "leaf"))
    top_solution = solve_top(top_rhs, merged, top_linv, top_uinv, top_mask)
    top_half = top_solution.astype(jnp.bfloat16)
    upper_local = upper_blocks[:, 0, 0]
    usum = lax.psum_scatter(
        jnp.einsum(
            "kjvw,kwn->jvn",
            upper_local * couple[:, :, None, None],
            top_half,
            preferred_element_type=jnp.float32,
        ),
        "row",
        scatter_dimension=0,
        tiled=True,
    )
    bottom_diff = ((bottom_y.astype(jnp.float32) - usum) * bottom_mask[..., None]).astype(
        jnp.bfloat16
    )
    bottom_solution = apply_blocks(bottom_uinv, bottom_diff) * bottom_mask[..., None]
    return (bottom_solution, top_solution)


def solution(mesh):
    placed = (
        P(("row", "col", "leaf"), None, None),
        P("row", None, None),
        P(("row", "col", "leaf"), None, None),
        P(("row", "col", "leaf"), None, None),
        P("row", None, None),
        P("row", None, None),
        P("row", "col", "leaf", None, None, None),
        P("row", "col", "leaf", None, None, None),
        P(("row", "col", "leaf")),
        P("row"),
        P("row", "col", "leaf", None),
        P("col", "leaf", None),
    )
    return jax.shard_map(
        local,
        mesh=mesh,
        in_specs=placed,
        out_specs=(P(("row", "col", "leaf"), None, None), P("row", None, None)),
        check_vma=False,
    )
```

profile of v0, /device:TPU:40, one launch (start us, length us, event | category | flops | bytes accessed | tf_op | source)
XLA Modules:
  0.0 253.4 jit_solution(489058026736499404)
XLA Ops:
  7.2 0.0 copy-start
  7.2 0.0 all-reduce.2.cloned.1.call-start
  8.0 1.2 fusion.3
  9.2 12.6 %all-gather = bf16[1024,128]{0,1:T(8,128)(2,1)S(1)} all-gather(bf16[256,128]{0,1:T(8,128)(2,1)S(1)} %bitcast.53), channel_id=2, replica_groups=mesh['row'=4,'col'=64,'leaf'=2] {'row'}, dimensions={0}, use_global_device_ids=true | all-gather | bytes 327680 | tf_op jit(solution)/shard_map/all_gather | solution.py:43
  21.8 0.2 copy.24
  22.0 0.0 copy-start.5
  22.0 0.7 copy-done.5
  22.7 0.7 copy-done.6
  23.3 0.1 fusion.22
  23.4 0.0 copy-done.8
  23.4 0.0 copy-start.3
  23.4 1.2 convolution_bitcast_fusion.1
  24.6 0.0 all-reduce.2.cloned.1.call-update
  24.7 0.0 reduce-scatter.2.cloned.1.call-start
  24.7 0.1 compare_convert_fusion
  24.8 190.9 %all-reduce.2.cloned.1.call-done = f32[2,256,128]{2,1,0:T(8,128)} async-done(((f32[2,256,128]{2,1,0:T(8,128)}), f32[2,256,128]{2,1,0:T(8,128)}) %all-reduce.2.cloned.1.call-update) | async-done | bytes 262160 | tf_op jit(solution)/shard_map/psum | solution.py:48
  215.7 1.4 fusion
  217.1 1.3 convolution_bitcast_fusion
  218.4 0.0 reduce-scatter.2.cloned.1.call-update
  218.4 0.0 copy-start.4
  218.5 0.8 copy.18
  219.3 25.4 %reduce-scatter.2.cloned.1.call-done = f32[1,256,128]{1,2,0:T(8,128)} async-done(((f32[4,256,128]{1,2,0:T(8,128)}), f32[1,256,128]{1,2,0:T(8,128)}) %reduce-scatter.2.cloned.1.call-update) | async-done | bytes 131088 | tf_op jit(solution)/shard_map/reduce_scatter | solution.py:52
  244.7 1.1 fusion.2
  245.8 0.8 copy.17
  (14 shorter events, 0.0 us)
Async XLA Ops:
  7.2 208.5 %copy-start = (bf16[2,256,256]{2,1,0:T(8,128)(2,1)S(1)}, bf16[2,256,256]{2,1,0:T(8,128)(2,1)}, u32[]{:S(2)}) copy-start(bf16[2,256,256]{2,1,0:T(8,128)(2,1)} %param.17) | copy-start | bytes 786436
  7.2 16.2 %copy-start.8 = (bf16[2,1,1,4,256,256]{5,4,3,2,1,0:T(8,128)(2,1)S(1)}, bf16[2,1,1,4,256,256]{5,4,3,2,1,0:T(8,128)(2,1)}, u32[]{:S(2)}) copy-start(bf16[2,1,1,4,256,256]{5,4,3,2,1,0:T(8,128)(2,1)} %param.18) | copy-start | bytes 3145732
  7.2 208.5 %all-reduce.2.cloned.1.call-start = ((), (), s32[]{:S(2)}) async-start(), calls=%async_computation.1 | async-start | bytes 524288 | tf_op jit(solution)/shard_map/psum | solution.py:48
  22.0 0.7 copy-start.5
  22.7 0.7 copy-start.6
  23.4 1.3 copy-start.7
  23.4 192.2 %copy-start.2 = (bf16[2,256,256]{2,1,0:T(8,128)(2,1)S(1)}, bf16[2,256,256]{2,1,0:T(8,128)(2,1)}, u32[]{:S(2)}) copy-start(bf16[2,256,256]{2,1,0:T(8,128)(2,1)} %param.16) | copy-start | bytes 786436
  23.4 192.2 %copy-start.3 = (bf16[2,256,128]{2,1,0:T(8,128)(2,1)S(1)}, bf16[2,256,128]{2,1,0:T(8,128)(2,1)}, u32[]{:S(2)}) copy-start(bf16[2,256,128]{2,1,0:T(8,128)(2,1)} %param.13) | copy-start | bytes 393220
  24.6 192.4 %copy-start.1 = (bf16[2,1,1,4,256,256]{5,4,3,2,1,0:T(8,128)(2,1)S(1)}, bf16[2,1,1,4,256,256]{5,4,3,2,1,0:T(8,128)(2,1)}, u32[]{:S(2)}) copy-start(bf16[2,1,1,4,256,256]{5,4,3,2,1,0:T(8,128)(2,1)} %param.19) | copy-start | bytes 3145732
  24.7 220.0 %reduce-scatter.2.cloned.1.call-start = ((), (), s32[]{:S(2)}) async-start(), calls=%async_computation.2 | async-start | bytes 655360 | tf_op jit(solution)/shard_map/reduce_scatter | solution.py:52
  218.4 26.3 %copy-start.4 = (bf16[1,256,256]{2,1,0:T(8,128)(2,1)S(1)}, bf16[1,256,256]{2,1,0:T(8,128)(2,1)}, u32[]{:S(2)}) copy-start(bf16[1,256,256]{2,1,0:T(8,128)(2,1)} %param.15) | copy-start | bytes 393220
Sparse Core Ops, SparseCore 0:
  24.8 190.8 all-reduce.1
  218.6 26.0 reduce-scatter.1
where the time goes:
time: 254 us; the launch traced here: 253 us
  waiting for transfers between devices  216 us (85%)
  between operations  14.9 us (6%)
  blocking collectives  12.6 us (5%)
  matrix products  6.26 us (2%)
  local copies, waits for them, and re-layouts  3.12 us (1%)
    psum x1, waiting for transfers between devices, local(): merged = lax.psum(partial_value, ('col', 'leaf'))  191 us
    reduce_scatter x1, waiting for transfers between devices, local(): lax.psum_scatter(jnp.einsum('kjvw,kwn->jvn', upper_local * couple[:, :, N...  25.4 us
    all_gather x1, blocking collectives, local(): column_values = lax.all_gather(bottom_y, 'row', axis=0, tiled=True)  12.6 us
  transfers between devices with their start and end apart: 2, of which 2 were waited for; matrix products, arithmetic and copies ran while one was open for 0% of the time, Pallas kernels for 0%

commit v1 on v0

v1 whole, which is shorter than its diff:
```python
import functools

import jax
import jax.numpy as jnp
from jax import lax
from jax.experimental import pallas as pl
from jax.experimental.pallas import tpu as pltpu
from jax.sharding import PartitionSpec as P

MESH = pl.DeviceIdType.MESH
F32 = jnp.float32
BF16 = jnp.bfloat16

W = 256
NRHS = 128
TPR = 2
NCB = 4
SIDE = 8
CHUNKS = 8
CH = TPR * W // CHUNKS

NEAR = ((0, 0), (0, 1), (-1, 0), (-1, 1), (-2, 0), (1, -1), (1, 0), (0, -1))
NEAR_ORDER = (4, 3, 5, 1, 2, 6, 7, 0)
FAR_ORDER = (2, 6, 3, 5, 4, 1, 7)
X_ORDER = (2, 1, 3)


def kernel(
    brhs_h,
    trhs_h,
    blinv_h,
    buinv_h,
    tlinv_h,
    tuinv_h,
    low_h,
    up_h,
    bw_ref,
    tw_ref,
    pat_ref,
    par_ref,
    bsol_ref,
    tsol_ref,
    brhs,
    trhs,
    blinv,
    buinv,
    tlinv,
    tuinv,
    low,
    up,
    ybuf,
    acc,
    part,
    rsbuf,
    midbuf,
    diff,
    ucon,
    ubuf,
    in_sem,
    xs_sem,
    xr_sem,
    rs_s,
    rs_r,
    mid_s,
    mid_r,
    ag_s,
    ag_r,
    us_s,
    us_r,
):
    row = lax.axis_index("row")
    col = lax.axis_index("col")
    leaf = lax.axis_index("leaf")
    z, y = lax.div(col, SIDE), lax.rem(col, SIDE)
    kind = lax.rem(y - 2 * z + 2 * SIDE, SIDE)

    def at(dz, dy, to_leaf):
        zz = lax.rem(z + (dz + SIDE), SIDE)
        yy = lax.rem(y + (dy + 2 * SIDE), SIDE)
        return (row, zz * SIDE + yy, to_leaf)

    def along(dx):
        return (lax.rem(row + dx, NCB), col, leaf)

    loads = []
    for i, (src, dst) in enumerate(
        (
            (blinv_h.at[0], blinv),
            (brhs_h.at[0], brhs),
            (low_h.at[:, 0, 0], low),
            (trhs_h, trhs),
            (tlinv_h, tlinv),
            (tuinv_h, tuinv),
            (up_h.at[:, 0, 0], up),
            (buinv_h.at[0], buinv),
        )
    ):
        load = pltpu.make_async_copy(src, dst, in_sem.at[i])
        load.start()
        loads.append(load)
    ld_blinv, ld_brhs, ld_low, ld_trhs, ld_tlinv, ld_tuinv, ld_up, ld_buinv = loads

    def hello(device):
        pl.semaphore_signal(barrier, inc=1, device_id=device, device_id_type=MESH)

    barrier = pltpu.get_barrier_semaphore()
    for dx in (1, 2, 3):
        hello(along(dx))
    for dz, dy in NEAR[1:]:
        hello(at(dz, dy, 1))

    @pl.when(leaf == 0)
    def _():
        hello(at(0, 0, 1))

    @pl.when(leaf == 1)
    def _():
        for dz, dy in NEAR:
            hello(at(-dz, -dy, 0))
        hello(at(2, 0, 1))
        for i in range(1, SIDE):
            hello(at(i, 2 * i, 1))

    places = lax.broadcasted_iota(jnp.int32, (W, NRHS), 0)
    bmask = places < bw_ref[0]

    def masked(value, mask):
        return jnp.where(mask, value, jnp.zeros_like(value))

    def dot(a, b):
        return jnp.dot(a, b, preferred_element_type=F32)

    ld_brhs.wait()
    ld_blinv.wait()
    rhs = masked(brhs[...].astype(F32), bmask).astype(BF16)
    own_y = masked(dot(blinv[...], rhs), bmask).astype(BF16)
    ybuf[row] = own_y

    pl.semaphore_wait(barrier, jnp.where(leaf == 1, 26, 11))

    xsends = []
    for dx in X_ORDER:
        send = pltpu.make_async_remote_copy(
            src_ref=ybuf.at[row],
            dst_ref=ybuf.at[row],
            send_sem=xs_sem.at[dx],
            recv_sem=xr_sem.at[dx],
            device_id=along(dx),
            device_id_type=MESH,
        )
        send.start()
        xsends.append(send)

    def couple(t, j):
        on = (pat_ref[t, 0, 0, j] > 0) | (par_ref[0, 0, j] == row * TPR + t)
        return jnp.where(on, 1.0, 0.0).astype(F32)

    def arrived(sem, dx, ref):
        pltpu.make_async_remote_copy(
            src_ref=ref,
            dst_ref=ref,
            send_sem=xs_sem.at[0],
            recv_sem=sem.at[dx],
            device_id=along(dx),
            device_id_type=MESH,
        ).wait_recv()

    ld_low.wait()
    for step, back in enumerate((0, 1, 3, 2)):
        j = lax.rem(row + NCB - back, NCB)
        if back:
            arrived(xr_sem, back, ybuf.at[j])
        vec = ybuf[j]
        for t in range(TPR):
            term = dot(low[t, j], vec) * couple(t, j)
            rows = pl.ds(t * W, W)
            if step == 0:
                acc[rows, :] = term
            elif step < NCB - 1:
                acc[rows, :] += term
            else:
                total = acc[rows, :] + term
                acc[rows, :] = total
                part[rows, :] = total.astype(BF16)

    def chunk(k):
        return pl.ds(pl.multiple_of(k * CH, CH), CH)

    def near_copy(m, to_leaf, slot):
        dz, dy = NEAR[m]
        k = lax.rem(kind + m, CHUNKS)
        return pltpu.make_async_remote_copy(
            src_ref=part.at[chunk(k)],
            dst_ref=rsbuf.at[slot],
            send_sem=rs_s.at[m],
            recv_sem=rs_r.at[slot],
            device_id=at(dz, dy, to_leaf),
            device_id_type=MESH,
        )

    @pl.when(leaf == 0)
    def _():
        for m in NEAR_ORDER:
            near_copy(m, 1, CHUNKS + m).start()

    own = chunk(kind)

    def back_copy(m, to_leaf):
        dz, dy = NEAR[m]
        return pltpu.make_async_remote_copy(
            src_ref=diff.at[own],
            dst_ref=diff.at[own],
            send_sem=ag_s.at[to_leaf, m],
            recv_sem=ag_r.at[m],
            device_id=at(-dz, -dy, to_leaf),
            device_id_type=MESH,
        )

    @pl.when(leaf == 1)
    def _():
        for m in NEAR_ORDER:
            if m:
                near_copy(m, 1, m).start()
        total = acc[own, :]
        for m in NEAR_ORDER:
            if m:
                near_copy(m, 1, m).wait_recv()
                total += rsbuf[m].astype(F32)
        for m in NEAR_ORDER:
            near_copy(m, 1, CHUNKS + m).wait_recv()
            total += rsbuf[CHUNKS + m].astype(F32)
        midbuf[z] = total.astype(BF16)

        fars = []
        for i in FAR_ORDER:
            far = pltpu.make_async_remote_copy(
                src_ref=midbuf.at[z],
                dst_ref=midbuf.at[z],
                send_sem=mid_s.at[i],
                recv_sem=mid_r.at[i],
                device_id=at(i, 2 * i, 1),
                device_id_type=MESH,
            )
            far.start()
            fars.append(far)
        ld_trhs.wait()
        for far in fars:
            far.wait_recv()
        lsum = midbuf[0].astype(F32)
        for i in range(1, SIDE):
            lsum += midbuf[i].astype(F32)
        top = lax.div(kind, CHUNKS // TPR)
        first = lax.rem(kind, CHUNKS // TPR) * CH
        here = lax.broadcasted_iota(jnp.int32, (CH, NRHS), 0) + first
        rest = trhs[top, pl.ds(pl.multiple_of(first, CH), CH), :].astype(F32) - lsum
        diff[own, :] = masked(rest, here < tw_ref[top]).astype(BF16)
        for to_leaf in (0, 1):
            for m in NEAR_ORDER:
                if m or to_leaf == 0:
                    back_copy(m, to_leaf).start()
        for far in fars:
            far.wait_send()
        for m in NEAR_ORDER:
            if m:
                near_copy(m, 1, m).wait_send()

    @pl.when(leaf == 0)
    def _():
        ld_trhs.wait()
        for m in NEAR_ORDER:
            near_copy(m, 1, CHUNKS + m).wait_send()
        back_copy(0, 0).wait_recv()

    for m in NEAR_ORDER:
        if m:
            back_copy(m, 0).wait_recv()

    ld_tlinv.wait()
    ld_tuinv.wait()
    halves = []
    for t in range(TPR):
        tmask = places < tw_ref[t]
        top_y = masked(dot(tlinv[t], diff[pl.ds(t * W, W), :]), tmask).astype(BF16)
        top = masked(dot(tuinv[t], top_y), tmask)
        tsol_ref[t] = top
        halves.append(top.astype(BF16))

    ld_up.wait()
    usends = []
    mine = None
    for dx in X_ORDER + (0,):
        j = lax.rem(row + dx, NCB)
        term = dot(up[0, j], halves[0]) * couple(0, j)
        term += dot(up[1, j], halves[1]) * couple(1, j)
        if dx == 0:
            mine = term
            break
        ucon[dx] = term.astype(BF16)
        send = pltpu.make_async_remote_copy(
            src_ref=ucon.at[dx],
            dst_ref=ubuf.at[dx],
            send_sem=us_s.at[dx],
            recv_sem=us_r.at[dx],
            device_id=along(dx),
            device_id_type=MESH,
        )
        send.start()
        usends.append(send)
    ld_buinv.wait()
    usum = mine
    for send, dx in zip(usends[1:] + usends[:1], (1, 3, 2)):
        send.wait_recv()
        usum += ubuf[dx].astype(F32)
    bdiff = masked(ybuf[row].astype(F32) - usum, bmask).astype(BF16)
    bsol_ref[0] = masked(dot(buinv[...], bdiff), bmask)

    for send in xsends + usends:
        send.wait_send()

    @pl.when(leaf == 1)
    def _():
        for to_leaf in (0, 1):
            for m in NEAR_ORDER:
                if m or to_leaf == 0:
                    back_copy(m, to_leaf).wait_send()


def local(*args):
    hbm = pl.BlockSpec(memory_space=pltpu.HBM)
    smem = pl.BlockSpec(memory_space=pltpu.SMEM)
    vmem = pl.BlockSpec(memory_space=pltpu.VMEM)
    dma = pltpu.SemaphoreType.DMA
    return pl.pallas_call(
        kernel,
        out_shape=(
            jax.ShapeDtypeStruct((1, W, NRHS), F32),
            jax.ShapeDtypeStruct((TPR, W, NRHS), F32),
        ),
        in_specs=[hbm] * 8 + [smem] * 4,
        out_specs=(vmem, vmem),
        scratch_shapes=[
            pltpu.VMEM((W, NRHS), BF16),
            pltpu.VMEM((TPR, W, NRHS), BF16),
            pltpu.VMEM((W, W), BF16),
            pltpu.VMEM((W, W), BF16),
            pltpu.VMEM((TPR, W, W), BF16),
            pltpu.VMEM((TPR, W, W), BF16),
            pltpu.VMEM((TPR, NCB, W, W), BF16),
            pltpu.VMEM((TPR, NCB, W, W), BF16),
            pltpu.VMEM((NCB, W, NRHS), BF16),
            pltpu.VMEM((TPR * W, NRHS), F32),
            pltpu.VMEM((TPR * W, NRHS), BF16),
            pltpu.VMEM((2 * CHUNKS, CH, NRHS), BF16),
            pltpu.VMEM((SIDE, CH, NRHS), BF16),
            pltpu.VMEM((TPR * W, NRHS), BF16),
            pltpu.VMEM((NCB, W, NRHS), BF16),
            pltpu.VMEM((NCB, W, NRHS), BF16),
            dma((8,)),
            dma((NCB,)),
            dma((NCB,)),
            dma((CHUNKS,)),
            dma((2 * CHUNKS,)),
            dma((SIDE,)),
            dma((SIDE,)),
            dma((2, CHUNKS)),
            dma((CHUNKS,)),
            dma((NCB,)),
            dma((NCB,)),
        ],
        compiler_params=pltpu.CompilerParams(
            collective_id=0, has_side_effects=True, vmem_limit_bytes=32 << 20
        ),
        name="substitution",
    )(*args)


def solution(mesh):
    placed = (
        P(("row", "col", "leaf"), None, None),
        P("row", None, None),
        P(("row", "col", "leaf"), None, None),
        P(("row", "col", "leaf"), None, None),
        P("row", None, None),
        P("row", None, None),
        P("row", "col", "leaf", None, None, None),
        P("row", "col", "leaf", None, None, None),
        P(("row", "col", "leaf")),
        P("row"),
        P("row", "col", "leaf", None),
        P("col", "leaf", None),
    )
    return jax.shard_map(
        local,
        mesh=mesh,
        in_specs=placed,
        out_specs=(P(("row", "col", "leaf"), None, None), P("row", None, None)),
        check_vma=False,
    )
```

time: 254 us -> 53.6 us (0.21)
  the two profiles are of different devices: /device:TPU:40 before, /device:TPU:1 now
where the time goes in v1:
time: 53.6 us; the launch traced here: 53.2 us
  Pallas kernels  41.9 us (78%)
  local copies, waits for them, and re-layouts  9.91 us (18%)
  between operations  1.36 us (3%)
    pallas_call x1, Pallas kernels, local(): pl.pallas_call(kernel, out_shape=(jax.ShapeDtypeStruct((1, W, NRHS), F32)...  41.9 us
    unnamed x24, local copies, waits for them, and re-layouts  9.91 us

profile of v1, /device:TPU:1, one launch (start us, length us, event | category | flops | bytes accessed | tf_op | source)
XLA Modules:
  0.0 53.2 jit_solution(13936062506980664421)
XLA Ops:
  0.6 0.0 copy-start.8
  0.6 0.0 copy-start.9
  1.3 0.0 copy-done.8
  1.3 0.0 copy-done.9
  1.3 0.0 copy-start
  1.3 1.2 %copy-done = bf16[2,1,1,4,256,256]{5,4,3,2,1,0:T(8,128)(2,1)S(1)} copy-done((bf16[2,1,1,4,256,256]{5,4,3,2,1,0:T(8,128)(2,1)S(1)}, bf16[2,1,1,4,256,256]{5,4,3,2,1,0:T(8,128)(2,1)}, u32[]{:S(2)}) %copy-start) | copy-done | bytes 1048600
  2.6 0.0 copy-start.1
  2.6 1.2 %copy-done.1 = bf16[2,1,1,4,256,256]{5,4,3,2,1,0:T(8,128)(2,1)S(1)} copy-done((bf16[2,1,1,4,256,256]{5,4,3,2,1,0:T(8,128)(2,1)S(1)}, bf16[2,1,1,4,256,256]{5,4,3,2,1,0:T(8,128)(2,1)}, u32[]{:S(2)}) %copy-start.1) | copy-done | bytes 1048600
  3.8 0.0 copy-start.2
  3.8 0.9 %copy-done.2 = bf16[2,256,256]{2,1,0:T(8,128)(2,1)S(1)} copy-done((bf16[2,256,256]{2,1,0:T(8,128)(2,1)S(1)}, bf16[2,256,256]{2,1,0:T(8,128)(2,1)}, u32[]{:S(2)}) %copy-start.2) | copy-done | bytes 262168
  4.7 0.0 copy-start.3
  4.7 0.9 %copy-done.3 = bf16[2,256,256]{2,1,0:T(8,128)(2,1)S(1)} copy-done((bf16[2,256,256]{2,1,0:T(8,128)(2,1)S(1)}, bf16[2,256,256]{2,1,0:T(8,128)(2,1)}, u32[]{:S(2)}) %copy-start.3) | copy-done | bytes 262168
  5.7 0.0 copy-start.4
  5.7 0.9 %copy-done.4 = bf16[2,256,128]{2,1,0:T(8,128)(2,1)S(1)} copy-done((bf16[2,256,128]{2,1,0:T(8,128)(2,1)S(1)}, bf16[2,256,128]{2,1,0:T(8,128)(2,1)}, u32[]{:S(2)}) %copy-start.4) | copy-done | bytes 131096
  6.6 0.0 copy-start.5
  6.6 0.9 %copy-done.5 = bf16[1,256,256]{2,1,0:T(8,128)(2,1)S(1)} copy-done((bf16[1,256,256]{2,1,0:T(8,128)(2,1)S(1)}, bf16[1,256,256]{2,1,0:T(8,128)(2,1)}, u32[]{:S(2)}) %copy-start.5) | copy-done | bytes 131096
  7.5 0.0 copy-start.6
  7.5 0.9 %copy-done.6 = bf16[1,256,256]{2,1,0:T(8,128)(2,1)S(1)} copy-done((bf16[1,256,256]{2,1,0:T(8,128)(2,1)S(1)}, bf16[1,256,256]{2,1,0:T(8,128)(2,1)}, u32[]{:S(2)}) %copy-start.6) | copy-done | bytes 131096
  8.4 0.0 copy-start.7
  8.4 0.8 %copy-done.7 = bf16[1,256,128]{2,1,0:T(8,128)(2,1)S(1)} copy-done((bf16[1,256,128]{2,1,0:T(8,128)(2,1)S(1)}, bf16[1,256,128]{2,1,0:T(8,128)(2,1)}, u32[]{:S(2)}) %copy-start.7) | copy-done | bytes 65560
  9.2 0.7 %copy-done.10 = s32[1,1,4]{2,1,0:T(1,128)S(1)} copy-done((s32[1,1,4]{2,1,0:T(1,128)S(1)}, s32[1,1,4]{2,1,0:T(1,128)}, u32[]{:S(2)}) %copy-start.10) | copy-done | bytes 40
  9.9 41.9 %substitution.1 = (f32[1,256,128]{2,1,0:T(8,128)S(1)}, f32[2,256,128]{2,1,0:T(8,128)S(1)}) custom-call(bf16[1,256,128]{2,1,0:T(8,128)(2,1)S(1)} %copy-done.7, bf16[2,256,128]{2,1,0:T(8,128)(2,1)S(1)} %copy-done.4, bf16[1,256,256]{2,1,0:T(8,128)(2,1)S(1)} %copy-done.5, bf16[1,256,256]{2,1,0:T(8,128)(2,1)S(1)} %copy-done.6, ...), custom_call_target="tpu_custom_call" | custom-call | tf_op jit(solution)/shard_map/substitution/pallas_call | solution.py:333
  51.8 0.7 %copy.17 = f32[1,256,128]{2,1,0:T(8,128)} copy(f32[1,256,128]{2,1,0:T(8,128)S(1)} %get-tuple-element.4) | data formatting | bytes 262144
  52.5 0.7 %copy.18 = f32[2,256,128]{2,1,0:T(8,128)} copy(f32[2,256,128]{2,1,0:T(8,128)S(1)} %get-tuple-element.5) | data formatting | bytes 524288
  (1 shorter events, 0.0 us)
Async XLA Ops:
  0.6 0.7 %copy-start.8 = (s32[2,1,1,4]{3,2,1,0:T(1,128)S(1)}, s32[2,1,1,4]{3,2,1,0:T(1,128)}, u32[]{:S(2)}) copy-start(s32[2,1,1,4]{3,2,1,0:T(1,128)} %pat_ref.1) | copy-start | bytes 100
  0.6 0.7 %copy-start.9 = (s32[2]{0:T(128)S(1)}, s32[2]{0:T(128)}, u32[]{:S(2)}) copy-start(s32[2]{0:T(128)} %tw_ref.1) | copy-start | bytes 28
  1.3 1.2 %copy-start = (bf16[2,1,1,4,256,256]{5,4,3,2,1,0:T(8,128)(2,1)S(1)}, bf16[2,1,1,4,256,256]{5,4,3,2,1,0:T(8,128)(2,1)}, u32[]{:S(2)}) copy-start(bf16[2,1,1,4,256,256]{5,4,3,2,1,0:T(8,128)(2,1)} %low_h.1) | copy-start | bytes 3145732
  2.6 1.2 %copy-start.1 = (bf16[2,1,1,4,256,256]{5,4,3,2,1,0:T(8,128)(2,1)S(1)}, bf16[2,1,1,4,256,256]{5,4,3,2,1,0:T(8,128)(2,1)}, u32[]{:S(2)}) copy-start(bf16[2,1,1,4,256,256]{5,4,3,2,1,0:T(8,128)(2,1)} %up_h.1) | copy-start | bytes 3145732
  3.8 0.9 %copy-start.2 = (bf16[2,256,256]{2,1,0:T(8,128)(2,1)S(1)}, bf16[2,256,256]{2,1,0:T(8,128)(2,1)}, u32[]{:S(2)}) copy-start(bf16[2,256,256]{2,1,0:T(8,128)(2,1)} %tlinv_h.1) | copy-start | bytes 786436
  4.7 0.9 %copy-start.3 = (bf16[2,256,256]{2,1,0:T(8,128)(2,1)S(1)}, bf16[2,256,256]{2,1,0:T(8,128)(2,1)}, u32[]{:S(2)}) copy-start(bf16[2,256,256]{2,1,0:T(8,128)(2,1)} %tuinv_h.1) | copy-start | bytes 786436
  5.7 0.9 %copy-start.4 = (bf16[2,256,128]{2,1,0:T(8,128)(2,1)S(1)}, bf16[2,256,128]{2,1,0:T(8,128)(2,1)}, u32[]{:S(2)}) copy-start(bf16[2,256,128]{2,1,0:T(8,128)(2,1)} %trhs_h.1) | copy-start | bytes 393220
  6.6 0.9 %copy-start.5 = (bf16[1,256,256]{2,1,0:T(8,128)(2,1)S(1)}, bf16[1,256,256]{2,1,0:T(8,128)(2,1)}, u32[]{:S(2)}) copy-start(bf16[1,256,256]{2,1,0:T(8,128)(2,1)} %blinv_h.1) | copy-start | bytes 393220
  7.5 0.9 %copy-start.6 = (bf16[1,256,256]{2,1,0:T(8,128)(2,1)S(1)}, bf16[1,256,256]{2,1,0:T(8,128)(2,1)}, u32[]{:S(2)}) copy-start(bf16[1,256,256]{2,1,0:T(8,128)(2,1)} %buinv_h.1) | copy-start | bytes 393220
  8.4 0.8 %copy-start.7 = (bf16[1,256,128]{2,1,0:T(8,128)(2,1)S(1)}, bf16[1,256,128]{2,1,0:T(8,128)(2,1)}, u32[]{:S(2)}) copy-start(bf16[1,256,128]{2,1,0:T(8,128)(2,1)} %brhs_h.1) | copy-start | bytes 196612
  9.2 0.7 %copy-start.10 = (s32[1,1,4]{2,1,0:T(1,128)S(1)}, s32[1,1,4]{2,1,0:T(1,128)}, u32[]{:S(2)}) copy-start(s32[1,1,4]{2,1,0:T(1,128)} %par_ref.1) | copy-start | bytes 52

commit v2 on v0

v2 whole, which is shorter than its diff:
```python
import jax
import jax.numpy as jnp
from jax import lax
from jax.experimental import pallas as pl
from jax.experimental.pallas import tpu as pltpu
from jax.sharding import PartitionSpec as P

MESH = pl.DeviceIdType.MESH
F32 = jnp.float32
BF16 = jnp.bfloat16

W = 256
NRHS = 128
TPR = 2
NCB = 4
SIDE = 8
PLANE = SIDE * SIDE
HUBS = SIDE
CH = TPR * W // HUBS

HUB_ORDER = (4, 3, 5, 2, 6, 1, 7, 0)
NEAR_FIRST = (0, 1, 7, 2, 6, 3, 5, 4)
ROWS = (1, 3, 0, 2)
LATE = 2


def kernel(
    brhs_h,
    trhs_h,
    blinv_h,
    buinv_h,
    tlinv_h,
    tuinv_h,
    low_h,
    up_h,
    bw_h,
    tw_h,
    pat_h,
    par_h,
    bsol_ref,
    tsol_ref,
    brhs,
    trhs,
    blinv,
    buinv,
    tlinv,
    tuinv,
    low,
    up,
    ybuf,
    acc,
    part,
    hubbuf,
    diff,
    ucon,
    ubuf,
    mine,
    cpl,
    bw_ref,
    tw_ref,
    pat_ref,
    par_ref,
    in_sem,
    pair_s,
    pair_r,
    xs_sem,
    xr_sem,
    hub_s,
    hub_r,
    out_s,
    out_r,
    us_s,
    us_r,
    late_sem,
):
    row = lax.axis_index("row")
    col = lax.axis_index("col")
    leaf = lax.axis_index("leaf")
    z, y = lax.div(col, SIDE), lax.rem(col, SIDE)
    late = row == LATE
    is_hub = z == 0

    def remote(src, dst, send_sem, recv_sem, device):
        return pltpu.make_async_remote_copy(
            src_ref=src,
            dst_ref=dst,
            send_sem=send_sem,
            recv_sem=recv_sem,
            device_id=device,
            device_id_type=MESH,
        )

    def load(i, src, dst):
        copy = pltpu.make_async_copy(src, dst, in_sem.at[i])
        copy.start()
        return copy

    barrier = pltpu.get_barrier_semaphore()

    def hello(device):
        pl.semaphore_signal(barrier, inc=1, device_id=device, device_id_type=MESH)

    def masked(value, mask):
        return jnp.where(mask, value, jnp.zeros_like(value))

    def dot(a, b):
        return jnp.dot(a, b, preferred_element_type=F32)

    places = lax.broadcasted_iota(jnp.int32, (W, NRHS), 0)

    def along(dx, to_leaf):
        return (lax.rem(row + dx, NCB), col, to_leaf)

    def own_y(ld_bw, ld_brhs, ld_blinv):
        ld_bw.wait()
        ld_brhs.wait()
        ld_blinv.wait()
        bmask = places < bw_ref[0]
        rhs = masked(brhs[...].astype(F32), bmask).astype(BF16)
        return bmask, masked(dot(blinv[...], rhs), bmask).astype(BF16)

    def couples(layer, ld_pat, ld_par):
        ld_pat.wait()
        ld_par.wait()
        for t in range(TPR):
            for j in range(NCB):
                on = (pat_ref[t, 0, 0, j] > 0) | (par_ref[0, 0, j] == row * TPR + t)
                cpl[layer, pl.ds(t * NCB + j, 1), :] = jnp.full(
                    (1, NRHS), jnp.where(on, 1.0, 0.0), F32
                )

    def finish(layer, bmask, own, ld_buinv):
        usum = jnp.zeros((W, NRHS), F32)
        for s in ROWS:

            @pl.when(s != row)
            def _():
                remote(
                    ubuf.at[s], ubuf.at[s], us_s.at[0, 0], us_r.at[s], along(1, layer)
                ).wait_recv()

            usum += jnp.where(s == row, own, ubuf[s].astype(F32))
        ld_buinv.wait()
        bdiff = masked(ybuf[layer, row].astype(F32) - usum, bmask).astype(BF16)
        bsol_ref[0] = masked(dot(buinv[...], bdiff), bmask)

    @pl.when(leaf == 0)
    def _():
        pair = (row, col, 1)
        ld_blinv = load(0, blinv_h.at[0], blinv)
        ld_brhs = load(1, brhs_h.at[0], brhs)
        ld_bw = load(2, bw_h, bw_ref)
        ld_pat = load(3, pat_h, pat_ref)
        ld_par = load(4, par_h, par_ref)
        ld_buinv = load(5, buinv_h.at[0], buinv)
        bmask, value = own_y(ld_bw, ld_brhs, ld_blinv)
        ybuf[0, row] = value
        couples(0, ld_pat, ld_par)
        pl.semaphore_wait(barrier, 1)
        sends = [
            remote(ybuf.at[0, row], ybuf.at[0, row], pair_s.at[0], pair_r.at[0], pair),
            remote(cpl.at[0], cpl.at[0], pair_s.at[1], pair_r.at[1], pair),
            remote(low_h.at[:, 0, 0], low.at[0], pair_s.at[2], pair_r.at[2], pair),
            remote(up_h.at[:, 0, 0], up.at[0], pair_s.at[3], pair_r.at[3], pair),
        ]
        for send in sends:
            send.start()
        for send in sends:
            send.wait_send()
        remote(mine, mine, pair_s.at[4], pair_r.at[4], pair).wait_recv()
        finish(0, bmask, mine[...], ld_buinv)
        remote(tsol_ref, tsol_ref, pair_s.at[5], pair_r.at[5], pair).wait_recv()

    def to_hub(h):
        rows = pl.ds(h * CH, CH)
        return remote(
            part.at[rows], hubbuf.at[col], hub_s.at[h], hub_r.at[col], (row, h, 1)
        )

    def hand(k, to_z, to_y):
        rows = pl.ds(pl.multiple_of(k * CH, CH), CH)
        return remote(
            diff.at[rows],
            diff.at[rows],
            out_s.at[lax.rem(z + SIDE - to_z, SIDE) if to_z is not z else SIDE + to_y],
            out_r.at[k],
            (row, to_z * SIDE + to_y, 1),
        )

    @pl.when(leaf == 1)
    def _():
        pair = (row, col, 0)
        ld_blinv = load(0, blinv_h.at[0], blinv)
        ld_brhs = load(1, brhs_h.at[0], brhs)
        ld_bw = load(2, bw_h, bw_ref)
        hello(pair)

        @pl.when(jnp.logical_not(late))
        def _():
            for dx in (2, 1, 3):
                hello(along(dx, 1))

        ld_pat = load(3, pat_h, pat_ref)
        ld_par = load(4, par_h, par_ref)
        ld_low = load(6, low_h.at[:, 0, 0], low.at[1])
        ld_tw = load(7, tw_h, tw_ref)
        ld_trhs = load(8, trhs_h, trhs)
        ld_tlinv = load(9, tlinv_h, tlinv)
        ld_tuinv = load(10, tuinv_h, tuinv)
        ld_up = load(11, up_h.at[:, 0, 0], up.at[1])
        ld_buinv = load(5, buinv_h.at[0], buinv)

        @pl.when(is_hub)
        def _():
            def greet(c, carry):
                @pl.when(c != col)
                def _():
                    hello((row, c, 1))

                return carry

            lax.fori_loop(0, PLANE, greet, 0)

        hubs = jnp.where(is_hub, HUBS - 1, HUBS)

        @pl.when(late)
        def _():
            pl.semaphore_wait(barrier, hubs + NCB - 1)
            for dx in (2, 1, 3):
                pl.semaphore_signal(
                    late_sem, inc=1, device_id=along(dx, 1), device_id_type=MESH
                )

        bmask, value = own_y(ld_bw, ld_brhs, ld_blinv)
        ybuf[1, row] = value

        @pl.when(jnp.logical_not(late))
        def _():
            pl.semaphore_wait(barrier, hubs + NCB - 2)

        def send_y(layer, to):
            return remote(
                ybuf.at[layer, row],
                ybuf.at[layer, row],
                xs_sem.at[layer, to],
                xr_sem.at[layer, row],
                (to, col, 1),
            )

        def wait_y0():
            remote(
                ybuf.at[0, row], ybuf.at[0, row], pair_s.at[0], pair_r.at[0], pair
            ).wait_recv()

        for layer in (1, 0):
            if layer == 0:
                wait_y0()
            for dx in (2, 1, 3):
                to = lax.rem(row + dx, NCB)

                @pl.when(late | (to != LATE))
                def _():
                    send_y(layer, to).start()

        @pl.when(jnp.logical_not(late))
        def _():
            pl.semaphore_wait(late_sem, 1)
            for layer in (1, 0):
                send_y(layer, LATE).start()

        couples(1, ld_pat, ld_par)
        ld_low.wait()
        remote(cpl.at[0], cpl.at[0], pair_s.at[1], pair_r.at[1], pair).wait_recv()
        remote(
            low_h.at[:, 0, 0], low.at[0], pair_s.at[2], pair_r.at[2], pair
        ).wait_recv()

        def factor(layer, t, j):
            return cpl[layer, pl.ds(t * NCB + j, 1), :]

        order = (
            row,
            jnp.where(lax.rem(row, 2) == 0, 1, 0),
            jnp.where(row == NCB - 1, 1, NCB - 1),
            jnp.where(late, 0, LATE),
        )
        steps = [(layer, i) for i in range(NCB) for layer in (1, 0)]
        for step, (layer, i) in enumerate(steps):
            s = order[i]
            if i:
                remote(
                    ybuf.at[layer, s],
                    ybuf.at[layer, s],
                    xs_sem.at[layer, s],
                    xr_sem.at[layer, s],
                    (s, col, 1),
                ).wait_recv()
            vec = ybuf[layer, s]
            if step < len(steps) - 1:
                for t in range(TPR):
                    term = dot(low[layer, t, s], vec) * factor(layer, t, s)
                    rows = pl.ds(t * W, W)
                    if step == 0:
                        acc[rows, :] = term
                    else:
                        acc[rows, :] += term
                continue
            for h in HUB_ORDER:
                t, first = h // (HUBS // TPR), h % (HUBS // TPR) * CH
                term = dot(low[layer, t, s, pl.ds(first, CH), :], vec)
                term *= factor(layer, t, s)
                rows = pl.ds(h * CH, CH)
                part[rows, :] = (acc[rows, :] + term).astype(BF16)

                @pl.when(col != h)
                def _():
                    to_hub(h).start()

        @pl.when(is_hub)
        def _():
            own = pl.ds(pl.multiple_of(y * CH, CH), CH)
            hubbuf[col] = part[own, :]

            def add(c, total):
                @pl.when(c != col)
                def _():
                    remote(
                        part.at[own], hubbuf.at[c], hub_s.at[0], hub_r.at[c], (row, c, 1)
                    ).wait_recv()

                return total + hubbuf[c].astype(F32)

            lsum = lax.fori_loop(0, PLANE, add, jnp.zeros((CH, NRHS), F32))
            ld_tw.wait()
            ld_trhs.wait()
            top = lax.div(y, HUBS // TPR)
            first = lax.rem(y, HUBS // TPR) * CH
            here = lax.broadcasted_iota(jnp.int32, (CH, NRHS), 0) + first
            width = jnp.where(top == 0, tw_ref[0], tw_ref[1])
            rest = trhs[top, pl.ds(pl.multiple_of(first, CH), CH), :].astype(F32) - lsum
            diff[own, :] = masked(rest, here < width).astype(BF16)

        @pl.when(jnp.logical_not(is_hub))
        def _():
            ld_tw.wait()
            ld_trhs.wait()
            hand(y, 0, y).wait_recv()

        for to in NEAR_FIRST:

            @pl.when(y != to)
            def _():
                hand(y, z, to).start()

        @pl.when(is_hub)
        def _():
            for to in NEAR_FIRST[1:]:
                hand(y, to, y).start()

        ld_tlinv.wait()
        ld_tuinv.wait()
        halves = []
        for t in range(TPR):
            for k in range(t * HUBS // TPR, (t + 1) * HUBS // TPR):

                @pl.when(y != k)
                def _():
                    hand(k, z, k).wait_recv()

            tmask = places < tw_ref[t]
            top_y = masked(dot(tlinv[t], diff[pl.ds(t * W, W), :]), tmask).astype(BF16)
            top = masked(dot(tuinv[t], top_y), tmask)
            tsol_ref[t] = top
            halves.append(top.astype(BF16))

        ld_up.wait()
        remote(up_h.at[:, 0, 0], up.at[0], pair_s.at[3], pair_r.at[3], pair).wait_recv()

        def contribution(layer, j):
            total = dot(up[layer, 0, j], halves[0]) * factor(layer, 0, j)
            return total + dot(up[layer, 1, j], halves[1]) * factor(layer, 1, j)

        sends = []
        for layer in (1, 0):
            for dx in (2, 1, 3):
                j = lax.rem(row + dx, NCB)
                ucon[layer, dx] = contribution(layer, j).astype(BF16)
                send = remote(
                    ucon.at[layer, dx],
                    ubuf.at[row],
                    us_s.at[layer, dx],
                    us_r.at[row],
                    (j, col, layer),
                )
                send.start()
                sends.append(send)
        mine[...] = contribution(0, row)
        sends.append(remote(mine, mine, pair_s.at[4], pair_r.at[4], pair))
        sends[-1].start()
        sends.append(remote(tsol_ref, tsol_ref, pair_s.at[5], pair_r.at[5], pair))
        sends[-1].start()
        own = contribution(1, row)

        finish(1, bmask, own, ld_buinv)
        for send in sends:
            send.wait_send()
        for layer in (1, 0):
            for dx in (1, 2, 3):
                send_y(layer, lax.rem(row + dx, NCB)).wait_send()
        for h in range(HUBS):

            @pl.when(col != h)
            def _():
                to_hub(h).wait_send()

            @pl.when(y != h)
            def _():
                hand(y, z, h).wait_send()

        @pl.when(is_hub)
        def _():
            for to in NEAR_FIRST[1:]:
                hand(y, to, y).wait_send()


def local(*args):
    hbm = pl.BlockSpec(memory_space=pltpu.HBM)
    vmem = pl.BlockSpec(memory_space=pltpu.VMEM)
    dma = pltpu.SemaphoreType.DMA
    return pl.pallas_call(
        kernel,
        out_shape=(
            pltpu.VMEM((1, W, NRHS), F32),
            pltpu.VMEM((TPR, W, NRHS), F32),
        ),
        in_specs=[hbm] * 12,
        out_specs=(vmem, vmem),
        scratch_shapes=[
            pltpu.VMEM((W, NRHS), BF16),
            pltpu.VMEM((TPR, W, NRHS), BF16),
            pltpu.VMEM((W, W), BF16),
            pltpu.VMEM((W, W), BF16),
            pltpu.VMEM((TPR, W, W), BF16),
            pltpu.VMEM((TPR, W, W), BF16),
            pltpu.VMEM((2, TPR, NCB, W, W), BF16),
            pltpu.VMEM((2, TPR, NCB, W, W), BF16),
            pltpu.VMEM((2, NCB, W, NRHS), BF16),
            pltpu.VMEM((TPR * W, NRHS), F32),
            pltpu.VMEM((TPR * W, NRHS), BF16),
            pltpu.VMEM((PLANE, CH, NRHS), BF16),
            pltpu.VMEM((TPR * W, NRHS), BF16),
            pltpu.VMEM((2, NCB, W, NRHS), BF16),
            pltpu.VMEM((NCB, W, NRHS), BF16),
            pltpu.VMEM((W, NRHS), F32),
            pltpu.VMEM((2, TPR * NCB, NRHS), F32),
            pltpu.SMEM((1,), jnp.int32),
            pltpu.SMEM((TPR,), jnp.int32),
            pltpu.SMEM((TPR, 1, 1, NCB), jnp.int32),
            pltpu.SMEM((1, 1, NCB), jnp.int32),
            dma((12,)),
            dma((6,)),
            dma((6,)),
            dma((2, NCB)),
            dma((2, NCB)),
            dma((HUBS,)),
            dma((PLANE,)),
            dma((2 * SIDE,)),
            dma((HUBS,)),
            dma((2, NCB)),
            dma((NCB,)),
            pltpu.SemaphoreType.REGULAR,
        ],
        compiler_params=pltpu.CompilerParams(
            collective_id=0, has_side_effects=True, vmem_limit_bytes=60 << 20
        ),
        name="substitution",
    )(*args)


def solution(mesh):
    placed = (
        P(("row", "col", "leaf"), None, None),
        P("row", None, None),
        P(("row", "col", "leaf"), None, None),
        P(("row", "col", "leaf"), None, None),
        P("row", None, None),
        P("row", None, None),
        P("row", "col", "leaf", None, None, None),
        P("row", "col", "leaf", None, None, None),
        P(("row", "col", "leaf")),
        P("row"),
        P("row", "col", "leaf", None),
        P("col", "leaf", None),
    )
    return jax.shard_map(
        local,
        mesh=mesh,
        in_specs=placed,
        out_specs=(P(("row", "col", "leaf"), None, None), P("row", None, None)),
        check_vma=False,
    )
```

time: 254 us -> 41.5 us (0.16)
  the two profiles are of different devices: /device:TPU:40 before, /device:TPU:64 now
where the time goes in v2:
time: 41.5 us; the launch traced here: 41.4 us
  Pallas kernels  38.7 us (93%)
  local copies, waits for them, and re-layouts  1.36 us (3%)
  between operations  1.29 us (3%)
    pallas_call x1, Pallas kernels, local(): pl.pallas_call(kernel, out_shape=(pltpu.VMEM((1, W, NRHS), F32), pltpu.VM...  38.7 us
    unnamed x2, local copies, waits for them, and re-layouts  1.36 us

profile of v2, /device:TPU:64, one launch (start us, length us, event | category | flops | bytes accessed | tf_op | source)
XLA Modules:
  0.0 41.4 jit_solution(4006084538749704654)
XLA Ops:
  1.3 38.7 %substitution.1 = (f32[1,256,128]{2,1,0:T(8,128)S(1)}, f32[2,256,128]{2,1,0:T(8,128)S(1)}) custom-call(bf16[1,256,128]{2,1,0:T(8,128)(2,1)} %brhs_h.1, bf16[2,256,128]{2,1,0:T(8,128)(2,1)} %trhs_h.1, bf16[1,256,256]{2,1,0:T(8,128)(2,1)} %blinv_h.1, bf16[1,256,256]{2,1,0:T(8,128)(2,1)} %buinv_h.1, bf16[2,256,256]{2,1,0:T(8,128)(2,1)} %tlinv_h.1, ...), custom_call_target="tpu_custom_call" | custom-call | tf_op jit(solution)/shard_map/substitution/pallas_call | solution.py:430
  40.0 0.7 %copy.16 = f32[1,256,128]{2,1,0:T(8,128)} copy(f32[1,256,128]{2,1,0:T(8,128)S(1)} %get-tuple-element.2) | data formatting | bytes 262144
  40.7 0.7 %copy.17 = f32[2,256,128]{2,1,0:T(8,128)} copy(f32[2,256,128]{2,1,0:T(8,128)S(1)} %get-tuple-element.3) | data formatting | bytes 524288

commit v3 on v2

--- a/solution.py
+++ b/solution.py
@@ -20,6 +20,18 @@
 
 HUB_ORDER = (4, 3, 5, 2, 6, 1, 7, 0)
 NEAR_FIRST = (0, 1, 7, 2, 6, 3, 5, 4)
+
+
+def chunk_of(hub):
+    if isinstance(hub, int):
+        return NEAR_FIRST.index(hub)
+    side = jnp.where(hub <= SIDE // 2, 2 * hub - 1, 2 * (SIDE - hub))
+    return jnp.where(hub == 0, 0, side)
+
+
+def chunk_rows(hub):
+    first = chunk_of(hub) * CH
+    return pl.ds(first if isinstance(first, int) else pl.multiple_of(first, CH), CH)
 ROWS = (1, 3, 0, 2)
 LATE = 2
 
@@ -172,17 +184,17 @@
         remote(tsol_ref, tsol_ref, pair_s.at[5], pair_r.at[5], pair).wait_recv()
 
     def to_hub(h):
-        rows = pl.ds(h * CH, CH)
+        rows = chunk_rows(h)
         return remote(
             part.at[rows], hubbuf.at[col], hub_s.at[h], hub_r.at[col], (row, h, 1)
         )
 
     def hand(k, to_z, to_y):
-        rows = pl.ds(pl.multiple_of(k * CH, CH), CH)
+        rows = chunk_rows(k)
         return remote(
             diff.at[rows],
             diff.at[rows],
-            out_s.at[lax.rem(z + SIDE - to_z, SIDE) if to_z is not z else SIDE + to_y],
+            out_s.at[to_z * SIDE + to_y],
             out_r.at[k],
             (row, to_z * SIDE + to_y, 1),
         )
@@ -190,46 +202,45 @@
     @pl.when(leaf == 1)
     def _():
         pair = (row, col, 0)
-        ld_blinv = load(0, blinv_h.at[0], blinv)
-        ld_brhs = load(1, brhs_h.at[0], brhs)
-        ld_bw = load(2, bw_h, bw_ref)
+        hubs = jnp.where(is_hub, HUBS - 1, HUBS)
         hello(pair)
+
+        @pl.when(is_hub)
+        def _():
+            def greet(c, carry):
+                @pl.when(c != col)
+                def _():
+                    hello((row, c, 1))
+
+                return carry
+
+            lax.fori_loop(0, PLANE, greet, 0)
+
+        @pl.when(late)
+        def _():
+            pl.semaphore_wait(barrier, hubs + NCB - 1)
+            for dx in (2, 1, 3):
+                pl.semaphore_signal(
+                    late_sem, inc=1, device_id=along(dx, 1), device_id_type=MESH
+                )
 
         @pl.when(jnp.logical_not(late))
         def _():
             for dx in (2, 1, 3):
                 hello(along(dx, 1))
 
+        ld_brhs = load(1, brhs_h.at[0], brhs)
+        ld_blinv = load(0, blinv_h.at[0], blinv)
+        ld_bw = load(2, bw_h, bw_ref)
+        ld_low = load(6, low_h.at[:, 0, 0], low.at[1])
         ld_pat = load(3, pat_h, pat_ref)
         ld_par = load(4, par_h, par_ref)
-        ld_low = load(6, low_h.at[:, 0, 0], low.at[1])
         ld_tw = load(7, tw_h, tw_ref)
         ld_trhs = load(8, trhs_h, trhs)
         ld_tlinv = load(9, tlinv_h, tlinv)
         ld_tuinv = load(10, tuinv_h, tuinv)
         ld_up = load(11, up_h.at[:, 0, 0], up.at[1])
         ld_buinv = load(5, buinv_h.at[0], buinv)
-
-        @pl.when(is_hub)
-        def _():
-            def greet(c, carry):
-                @pl.when(c != col)
-                def _():
-                    hello((row, c, 1))
-
-                return carry
-
-            lax.fori_loop(0, PLANE, greet, 0)
-
-        hubs = jnp.where(is_hub, HUBS - 1, HUBS)
-
-        @pl.when(late)
-        def _():
-            pl.semaphore_wait(barrier, hubs + NCB - 1)
-            for dx in (2, 1, 3):
-                pl.semaphore_signal(
-                    late_sem, inc=1, device_id=along(dx, 1), device_id_type=MESH
-                )
 
         bmask, value = own_y(ld_bw, ld_brhs, ld_blinv)
         ybuf[1, row] = value
@@ -251,6 +262,15 @@
             remote(
                 ybuf.at[0, row], ybuf.at[0, row], pair_s.at[0], pair_r.at[0], pair
             ).wait_recv()
+
+        def arrived(layer, s):
+            return remote(
+                ybuf.at[layer, s],
+                ybuf.at[layer, s],
+                xs_sem.at[layer, s],
+                xr_sem.at[layer, s],
+                (s, col, 1),
+            )
 
         for layer in (1, 0):
             if layer == 0:
@@ -288,13 +308,7 @@
         for step, (layer, i) in enumerate(steps):
             s = order[i]
             if i:
-                remote(
-                    ybuf.at[layer, s],
-                    ybuf.at[layer, s],
-                    xs_sem.at[layer, s],
-                    xr_sem.at[layer, s],
-                    (s, col, 1),
-                ).wait_recv()
+                arrived(layer, s).wait_recv()
             vec = ybuf[layer, s]
             if step < len(steps) - 1:
                 for t in range(TPR):
@@ -306,10 +320,10 @@
                         acc[rows, :] += term
                 continue
             for h in HUB_ORDER:
-                t, first = h // (HUBS // TPR), h % (HUBS // TPR) * CH
+                t, first = divmod(chunk_of(h) * CH, W)
                 term = dot(low[layer, t, s, pl.ds(first, CH), :], vec)
                 term *= factor(layer, t, s)
-                rows = pl.ds(h * CH, CH)
+                rows = chunk_rows(h)
                 part[rows, :] = (acc[rows, :] + term).astype(BF16)
 
                 @pl.when(col != h)
@@ -318,7 +332,7 @@
 
         @pl.when(is_hub)
         def _():
-            own = pl.ds(pl.multiple_of(y * CH, CH), CH)
+            own = chunk_rows(y)
             hubbuf[col] = part[own, :]
 
             def add(c, total):
@@ -333,8 +347,8 @@
             lsum = lax.fori_loop(0, PLANE, add, jnp.zeros((CH, NRHS), F32))
             ld_tw.wait()
             ld_trhs.wait()
-            top = lax.div(y, HUBS // TPR)
-            first = lax.rem(y, HUBS // TPR) * CH
+            top = lax.div(chunk_of(y), HUBS // TPR)
+            first = lax.rem(chunk_of(y), HUBS // TPR) * CH
             here = lax.broadcasted_iota(jnp.int32, (CH, NRHS), 0) + first
             width = jnp.where(top == 0, tw_ref[0], tw_ref[1])
             rest = trhs[top, pl.ds(pl.multiple_of(first, CH), CH), :].astype(F32) - lsum
@@ -346,29 +360,42 @@
             ld_trhs.wait()
             hand(y, 0, y).wait_recv()
 
-        for to in NEAR_FIRST:
-
-            @pl.when(y != to)
+        def to_lines(do, first, last):
+            @pl.when(is_hub)
             def _():
-                hand(y, z, to).start()
-
-        @pl.when(is_hub)
-        def _():
-            for to in NEAR_FIRST[1:]:
-                hand(y, to, y).start()
+                for to_z in range(first, last):
+                    do(hand(y, to_z, y))
+
+        def to_line(do):
+            for to in NEAR_FIRST:
+
+                @pl.when(y != to)
+                def _():
+                    do(hand(y, z, to))
+
+        to_lines(lambda copy: copy.start(), 1, 2)
+        to_line(lambda copy: copy.start())
+        to_lines(lambda copy: copy.start(), 2, SIDE)
 
         ld_tlinv.wait()
         ld_tuinv.wait()
         halves = []
         for t in range(TPR):
-            for k in range(t * HUBS // TPR, (t + 1) * HUBS // TPR):
-
-                @pl.when(y != k)
-                def _():
-                    hand(k, z, k).wait_recv()
-
+            total = None
+            for part_of in range(2):
+                first = t * HUBS // TPR + part_of * 2
+                for k in NEAR_FIRST[first : first + 2]:
+
+                    @pl.when(y != k)
+                    def _():
+                        hand(k, z, k).wait_recv()
+
+                rows = pl.ds(first * CH, 2 * CH)
+                inner = pl.ds(part_of * 2 * CH, 2 * CH)
+                term = dot(tlinv[t, :, inner], diff[rows, :])
+                total = term if total is None else total + term
             tmask = places < tw_ref[t]
-            top_y = masked(dot(tlinv[t], diff[pl.ds(t * W, W), :]), tmask).astype(BF16)
+            top_y = masked(total, tmask).astype(BF16)
             top = masked(dot(tuinv[t], top_y), tmask)
             tsol_ref[t] = top
             halves.append(top.astype(BF16))
@@ -381,23 +408,22 @@
             return total + dot(up[layer, 1, j], halves[1]) * factor(layer, 1, j)
 
         sends = []
-        for layer in (1, 0):
-            for dx in (2, 1, 3):
-                j = lax.rem(row + dx, NCB)
-                ucon[layer, dx] = contribution(layer, j).astype(BF16)
-                send = remote(
-                    ucon.at[layer, dx],
-                    ubuf.at[row],
-                    us_s.at[layer, dx],
-                    us_r.at[row],
-                    (j, col, layer),
-                )
-                send.start()
-                sends.append(send)
+        for layer, dx in ((1, 2), (1, 1), (1, 3), (0, 2), (0, 1), (0, 3)):
+            j = lax.rem(row + dx, NCB)
+            ucon[layer, dx] = contribution(layer, j).astype(BF16)
+            send = remote(
+                ucon.at[layer, dx],
+                ubuf.at[row],
+                us_s.at[layer, dx],
+                us_r.at[row],
+                (j, col, layer),
+            )
+            send.start()
+            sends.append(send)
+        sends.append(remote(tsol_ref, tsol_ref, pair_s.at[5], pair_r.at[5], pair))
+        sends[-1].start()
         mine[...] = contribution(0, row)
         sends.append(remote(mine, mine, pair_s.at[4], pair_r.at[4], pair))
-        sends[-1].start()
-        sends.append(remote(tsol_ref, tsol_ref, pair_s.at[5], pair_r.at[5], pair))
         sends[-1].start()
         own = contribution(1, row)
 
@@ -406,28 +432,35 @@
             send.wait_send()
         for layer in (1, 0):
             for dx in (1, 2, 3):
-                send_y(layer, lax.rem(row + dx, NCB)).wait_send()
+                to = lax.rem(row + dx, NCB)
+
+                send_y(layer, to).wait_send()
         for h in range(HUBS):
 
             @pl.when(col != h)
             def _():
                 to_hub(h).wait_send()
 
-            @pl.when(y != h)
-            def _():
-                hand(y, z, h).wait_send()
-
-        @pl.when(is_hub)
-        def _():
-            for to in NEAR_FIRST[1:]:
-                hand(y, to, y).wait_send()
+        to_line(lambda copy: copy.wait_send())
+        to_lines(lambda copy: copy.wait_send(), 1, SIDE)
+
+
+def write(bsol, tsol, bsol_h, tsol_h, sem):
+    copies = [
+        pltpu.make_async_copy(tsol, tsol_h, sem.at[0]),
+        pltpu.make_async_copy(bsol, bsol_h, sem.at[1]),
+    ]
+    for copy in copies:
+        copy.start()
+    for copy in copies:
+        copy.wait()
 
 
 def local(*args):
     hbm = pl.BlockSpec(memory_space=pltpu.HBM)
     vmem = pl.BlockSpec(memory_space=pltpu.VMEM)
     dma = pltpu.SemaphoreType.DMA
-    return pl.pallas_call(
+    solved = pl.pallas_call(
         kernel,
         out_shape=(
             pltpu.VMEM((1, W, NRHS), F32),
@@ -464,7 +497,7 @@
             dma((2, NCB)),
             dma((HUBS,)),
             dma((PLANE,)),
-            dma((2 * SIDE,)),
+            dma((PLANE,)),
             dma((HUBS,)),
             dma((2, NCB)),
             dma((NCB,)),
@@ -475,6 +508,17 @@
         ),
         name="substitution",
     )(*args)
+    return pl.pallas_call(
+        write,
+        out_shape=(
+            jax.ShapeDtypeStruct((1, W, NRHS), F32),
+            jax.ShapeDtypeStruct((TPR, W, NRHS), F32),
+        ),
+        in_specs=[pl.BlockSpec(memory_space=pl.ANY)] * 2,
+        out_specs=(hbm, hbm),
+        scratch_shapes=[dma((2,))],
+        name="write",
+    )(*[pltpu.with_memory_space_constraint(v, pltpu.VMEM) for v in solved])
 
 
 def solution(mesh):

time: 41.5 us -> 41.3 us (level)
  local copies, waits for them, and re-layouts: 1.36 us -> 0 us
  Pallas kernels: 38.7 us -> 39.8 us
    unnamed x2 -> x0, local copies, waits for them, and re-layouts: 1.36 us -> none
    pallas_call x0 -> x1, Pallas kernels: none -> 0.76 us  [local(): pl.pallas_call(write, out_shape=(jax.ShapeDtypeStruct((1, W, NRHS), F32),...]
where the time goes in v3:
time: 41.3 us; the launch traced here: 41.1 us
  Pallas kernels  39.8 us (96%)
  between operations  1.29 us (3%)
    pallas_call x1, Pallas kernels, local(): pl.pallas_call(kernel, out_shape=(pltpu.VMEM((1, W, NRHS), F32), pltpu.VM...  39.1 us

profile of v3, /device:TPU:64, one launch (start us, length us, event | category | flops | bytes accessed | tf_op | source)
XLA Modules:
  0.0 41.1 jit_solution(1395244784578312369)
XLA Ops:
  1.3 39.1 %substitution.1 = (f32[1,256,128]{2,1,0:T(8,128)S(1)}, f32[2,256,128]{2,1,0:T(8,128)S(1)}) custom-call(bf16[1,256,128]{2,1,0:T(8,128)(2,1)} %brhs_h.1, bf16[2,256,128]{2,1,0:T(8,128)(2,1)} %trhs_h.1, bf16[1,256,256]{2,1,0:T(8,128)(2,1)} %blinv_h.1, bf16[1,256,256]{2,1,0:T(8,128)(2,1)} %buinv_h.1, bf16[2,256,256]{2,1,0:T(8,128)(2,1)} %tlinv_h.1, ...), custom_call_target="tpu_custom_call" | custom-call | tf_op jit(solution)/shard_map/substitution/pallas_call | solution.py:463
  40.4 0.8 %write.1 = (f32[1,256,128]{2,1,0:T(8,128)}, f32[2,256,128]{2,1,0:T(8,128)}) custom-call(f32[1,256,128]{2,1,0:T(8,128)S(1)} %get-tuple-element.4.bsol, f32[2,256,128]{2,1,0:T(8,128)S(1)} %get-tuple-element.5.tsol), custom_call_target="tpu_custom_call" | custom-call | tf_op jit(solution)/shard_map/write/pallas_call | solution.py:511

commit v4 on v3

--- a/solution.py
+++ b/solution.py
@@ -83,7 +83,6 @@
     out_r,
     us_s,
     us_r,
-    late_sem,
 ):
     row = lax.axis_index("row")
     col = lax.axis_index("col")
@@ -167,7 +166,6 @@
         ld_buinv = load(5, buinv_h.at[0], buinv)
         bmask, value = own_y(ld_bw, ld_brhs, ld_blinv)
         ybuf[0, row] = value
-        couples(0, ld_pat, ld_par)
         pl.semaphore_wait(barrier, 1)
         sends = [
             remote(ybuf.at[0, row], ybuf.at[0, row], pair_s.at[0], pair_r.at[0], pair),
@@ -175,7 +173,9 @@
             remote(low_h.at[:, 0, 0], low.at[0], pair_s.at[2], pair_r.at[2], pair),
             remote(up_h.at[:, 0, 0], up.at[0], pair_s.at[3], pair_r.at[3], pair),
         ]
-        for send in sends:
+        sends[0].start()
+        couples(0, ld_pat, ld_par)
+        for send in sends[1:]:
             send.start()
         for send in sends:
             send.wait_send()
@@ -205,6 +205,13 @@
         hubs = jnp.where(is_hub, HUBS - 1, HUBS)
         hello(pair)
 
+        for dx in (2, 1, 3):
+            hello(along(dx, 1))
+
+        ld_brhs = load(1, brhs_h.at[0], brhs)
+        ld_blinv = load(0, blinv_h.at[0], blinv)
+        ld_bw = load(2, bw_h, bw_ref)
+
         @pl.when(is_hub)
         def _():
             def greet(c, carry):
@@ -216,22 +223,52 @@
 
             lax.fori_loop(0, PLANE, greet, 0)
 
+        bmask, value = own_y(ld_bw, ld_brhs, ld_blinv)
+        ybuf[1, row] = value
+
+        pl.semaphore_wait(barrier, hubs + NCB - 1)
+
+        def send_y(layer, to):
+            return remote(
+                ybuf.at[layer, row],
+                ybuf.at[layer, row],
+                xs_sem.at[layer, to],
+                xr_sem.at[layer, row],
+                (to, col, 1),
+            )
+
+        def wait_y0():
+            remote(
+                ybuf.at[0, row], ybuf.at[0, row], pair_s.at[0], pair_r.at[0], pair
+            ).wait_recv()
+
+        def arrived(layer, s):
+            return remote(
+                ybuf.at[layer, s],
+                ybuf.at[layer, s],
+                xs_sem.at[layer, s],
+                xr_sem.at[layer, s],
+                (s, col, 1),
+            )
+
+        def send_to_others(layer):
+            for dx in (2, 1, 3):
+                to = lax.rem(row + dx, NCB)
+
+                @pl.when(late | (to != LATE))
+                def _():
+                    send_y(layer, to).start()
+
+        def send_to_late(layer):
+            @pl.when(jnp.logical_not(late))
+            def _():
+                send_y(layer, LATE).start()
+
         @pl.when(late)
         def _():
-            pl.semaphore_wait(barrier, hubs + NCB - 1)
-            for dx in (2, 1, 3):
-                pl.semaphore_signal(
-                    late_sem, inc=1, device_id=along(dx, 1), device_id_type=MESH
-                )
-
-        @pl.when(jnp.logical_not(late))
-        def _():
-            for dx in (2, 1, 3):
-                hello(along(dx, 1))
-
-        ld_brhs = load(1, brhs_h.at[0], brhs)
-        ld_blinv = load(0, blinv_h.at[0], blinv)
-        ld_bw = load(2, bw_h, bw_ref)
+            send_to_others(1)
+
+        send_to_late(1)
         ld_low = load(6, low_h.at[:, 0, 0], low.at[1])
         ld_pat = load(3, pat_h, pat_ref)
         ld_par = load(4, par_h, par_ref)
@@ -241,52 +278,14 @@
         ld_tuinv = load(10, tuinv_h, tuinv)
         ld_up = load(11, up_h.at[:, 0, 0], up.at[1])
         ld_buinv = load(5, buinv_h.at[0], buinv)
-
-        bmask, value = own_y(ld_bw, ld_brhs, ld_blinv)
-        ybuf[1, row] = value
+        wait_y0()
+        send_to_late(0)
 
         @pl.when(jnp.logical_not(late))
         def _():
-            pl.semaphore_wait(barrier, hubs + NCB - 2)
-
-        def send_y(layer, to):
-            return remote(
-                ybuf.at[layer, row],
-                ybuf.at[layer, row],
-                xs_sem.at[layer, to],
-                xr_sem.at[layer, row],
-                (to, col, 1),
-            )
-
-        def wait_y0():
-            remote(
-                ybuf.at[0, row], ybuf.at[0, row], pair_s.at[0], pair_r.at[0], pair
-            ).wait_recv()
-
-        def arrived(layer, s):
-            return remote(
-                ybuf.at[layer, s],
-                ybuf.at[layer, s],
-                xs_sem.at[layer, s],
-                xr_sem.at[layer, s],
-                (s, col, 1),
-            )
-
-        for layer in (1, 0):
-            if layer == 0:
-                wait_y0()
-            for dx in (2, 1, 3):
-                to = lax.rem(row + dx, NCB)
-
-                @pl.when(late | (to != LATE))
-                def _():
-                    send_y(layer, to).start()
-
-        @pl.when(jnp.logical_not(late))
-        def _():
-            pl.semaphore_wait(late_sem, 1)
-            for layer in (1, 0):
-                send_y(layer, LATE).start()
+            send_to_others(1)
+
+        send_to_others(0)
 
         couples(1, ld_pat, ld_par)
         ld_low.wait()
@@ -319,8 +318,10 @@
                     else:
                         acc[rows, :] += term
                 continue
-            for h in HUB_ORDER:
-                t, first = divmod(chunk_of(h) * CH, W)
+            for step in HUB_ORDER:
+                h = lax.rem(y + step, HUBS)
+                t = lax.div(chunk_of(h), HUBS // TPR)
+                first = pl.multiple_of(lax.rem(chunk_of(h), HUBS // TPR) * CH, CH)
                 term = dot(low[layer, t, s, pl.ds(first, CH), :], vec)
                 term *= factor(layer, t, s)
                 rows = chunk_rows(h)
@@ -408,7 +409,7 @@
             return total + dot(up[layer, 1, j], halves[1]) * factor(layer, 1, j)
 
         sends = []
-        for layer, dx in ((1, 2), (1, 1), (1, 3), (0, 2), (0, 1), (0, 3)):
+        for layer, dx in ((1, 2), (1, 3), (1, 1), (0, 2), (0, 3), (0, 1)):
             j = lax.rem(row + dx, NCB)
             ucon[layer, dx] = contribution(layer, j).astype(BF16)
             send = remote(
@@ -427,22 +428,23 @@
         sends[-1].start()
         own = contribution(1, row)
 
+        for layer in (1, 0):
+            for dx in (1, 2, 3):
+                to = lax.rem(row + dx, NCB)
+
+                send_y(layer, to).wait_send()
+        for h in range(HUBS):
+
+            @pl.when(col != h)
+            def _():
+                to_hub(h).wait_send()
+
+        to_line(lambda copy: copy.wait_send())
+        to_lines(lambda copy: copy.wait_send(), 1, SIDE)
+
         finish(1, bmask, own, ld_buinv)
         for send in sends:
             send.wait_send()
-        for layer in (1, 0):
-            for dx in (1, 2, 3):
-                to = lax.rem(row + dx, NCB)
-
-                send_y(layer, to).wait_send()
-        for h in range(HUBS):
-
-            @pl.when(col != h)
-            def _():
-                to_hub(h).wait_send()
-
-        to_line(lambda copy: copy.wait_send())
-        to_lines(lambda copy: copy.wait_send(), 1, SIDE)
 
 
 def write(bsol, tsol, bsol_h, tsol_h, sem):
@@ -501,10 +503,9 @@
             dma((HUBS,)),
             dma((2, NCB)),
             dma((NCB,)),
-            pltpu.SemaphoreType.REGULAR,
         ],
         compiler_params=pltpu.CompilerParams(
-            collective_id=0, has_side_effects=True, vmem_limit_bytes=60 << 20
+            collective_id=0, has_side_effects=True, vmem_limit_bytes=56 << 20
         ),
         name="substitution",
     )(*args)

time: 41.3 us -> 41 us (level)
  no operation moved by 1% of the time
where the time goes in v4:
time: 41 us; the launch traced here: 40.9 us
  Pallas kernels  39.6 us (97%)
  between operations  1.29 us (3%)
    pallas_call x1, Pallas kernels, local(): pl.pallas_call(kernel, out_shape=(pltpu.VMEM((1, W, NRHS), F32), pltpu.VM...  38.8 us

profile of v4, /device:TPU:64, one launch (start us, length us, event | category | flops | bytes accessed | tf_op | source)
XLA Modules:
  0.0 40.9 jit_solution(10494121547165854246)
XLA Ops:
  1.3 38.8 %substitution.1 = (f32[1,256,128]{2,1,0:T(8,128)S(1)}, f32[2,256,128]{2,1,0:T(8,128)S(1)}) custom-call(bf16[1,256,128]{2,1,0:T(8,128)(2,1)} %brhs_h.1, bf16[2,256,128]{2,1,0:T(8,128)(2,1)} %trhs_h.1, bf16[1,256,256]{2,1,0:T(8,128)(2,1)} %blinv_h.1, bf16[1,256,256]{2,1,0:T(8,128)(2,1)} %buinv_h.1, bf16[2,256,256]{2,1,0:T(8,128)(2,1)} %tlinv_h.1, ...), custom_call_target="tpu_custom_call" | custom-call | tf_op jit(solution)/shard_map/substitution/pallas_call | solution.py:465
  40.1 0.8 %write.1 = (f32[1,256,128]{2,1,0:T(8,128)}, f32[2,256,128]{2,1,0:T(8,128)}) custom-call(f32[1,256,128]{2,1,0:T(8,128)S(1)} %get-tuple-element.4.bsol, f32[2,256,128]{2,1,0:T(8,128)S(1)} %get-tuple-element.5.tsol), custom_call_target="tpu_custom_call" | custom-call | tf_op jit(solution)/shard_map/write/pallas_call | solution.py:512

commit v5 on v4

--- a/solution.py
+++ b/solution.py
@@ -18,6 +18,7 @@
 HUBS = SIDE
 CH = TPR * W // HUBS
 
+HUB_Z = 1
 HUB_ORDER = (4, 3, 5, 2, 6, 1, 7, 0)
 NEAR_FIRST = (0, 1, 7, 2, 6, 3, 5, 4)
 
@@ -89,7 +90,7 @@
     leaf = lax.axis_index("leaf")
     z, y = lax.div(col, SIDE), lax.rem(col, SIDE)
     late = row == LATE
-    is_hub = z == 0
+    is_hub = z == HUB_Z
 
     def remote(src, dst, send_sem, recv_sem, device):
         return pltpu.make_async_remote_copy(
@@ -186,7 +187,11 @@
     def to_hub(h):
         rows = chunk_rows(h)
         return remote(
-            part.at[rows], hubbuf.at[col], hub_s.at[h], hub_r.at[col], (row, h, 1)
+            part.at[rows],
+            hubbuf.at[col],
+            hub_s.at[h],
+            hub_r.at[col],
+            (row, HUB_Z * SIDE + h, 1),
         )
 
     def hand(k, to_z, to_y):
@@ -327,7 +332,7 @@
                 rows = chunk_rows(h)
                 part[rows, :] = (acc[rows, :] + term).astype(BF16)
 
-                @pl.when(col != h)
+                @pl.when(col != HUB_Z * SIDE + h)
                 def _():
                     to_hub(h).start()
 
@@ -359,24 +364,30 @@
         def _():
             ld_tw.wait()
             ld_trhs.wait()
-            hand(y, 0, y).wait_recv()
-
-        def to_lines(do, first, last):
+            hand(y, z, y).wait_recv()
+
+        def to_root_line(do):
             @pl.when(is_hub)
             def _():
-                for to_z in range(first, last):
+                for to in NEAR_FIRST:
+                    do(hand(y, 0, to))
+
+        def to_columns(do):
+            @pl.when(is_hub)
+            def _():
+                for to_z in range(HUB_Z + 1, SIDE):
                     do(hand(y, to_z, y))
 
         def to_line(do):
             for to in NEAR_FIRST:
 
-                @pl.when(y != to)
+                @pl.when((y != to) & (z > 0))
                 def _():
                     do(hand(y, z, to))
 
-        to_lines(lambda copy: copy.start(), 1, 2)
+        to_root_line(lambda copy: copy.start())
         to_line(lambda copy: copy.start())
-        to_lines(lambda copy: copy.start(), 2, SIDE)
+        to_columns(lambda copy: copy.start())
 
         ld_tlinv.wait()
         ld_tuinv.wait()
@@ -435,12 +446,13 @@
                 send_y(layer, to).wait_send()
         for h in range(HUBS):
 
-            @pl.when(col != h)
+            @pl.when(col != HUB_Z * SIDE + h)
             def _():
                 to_hub(h).wait_send()
 
         to_line(lambda copy: copy.wait_send())
-        to_lines(lambda copy: copy.wait_send(), 1, SIDE)
+        to_root_line(lambda copy: copy.wait_send())
+        to_columns(lambda copy: copy.wait_send())
 
         finish(1, bmask, own, ld_buinv)
         for send in sends:

time: 41 us -> 38.7 us (0.944)
  the two profiles are of different devices: /device:TPU:64 before, /device:TPU:56 now
where the time goes in v5:
time: 38.7 us; the launch traced here: 38.6 us
  Pallas kernels  37.3 us (96%)
  between operations  1.29 us (3%)
    pallas_call x1, Pallas kernels, local(): pl.pallas_call(kernel, out_shape=(pltpu.VMEM((1, W, NRHS), F32), pltpu.VM...  36.5 us

profile of v5, /device:TPU:56, one launch (start us, length us, event | category | flops | bytes accessed | tf_op | source)
XLA Modules:
  0.0 38.6 jit_solution(3211661499488867195)
XLA Ops:
  1.3 36.5 %substitution.1 = (f32[1,256,128]{2,1,0:T(8,128)S(1)}, f32[2,256,128]{2,1,0:T(8,128)S(1)}) custom-call(bf16[1,256,128]{2,1,0:T(8,128)(2,1)} %brhs_h.1, bf16[2,256,128]{2,1,0:T(8,128)(2,1)} %trhs_h.1, bf16[1,256,256]{2,1,0:T(8,128)(2,1)} %blinv_h.1, bf16[1,256,256]{2,1,0:T(8,128)(2,1)} %buinv_h.1, bf16[2,256,256]{2,1,0:T(8,128)(2,1)} %tlinv_h.1, ...), custom_call_target="tpu_custom_call" | custom-call | tf_op jit(solution)/shard_map/substitution/pallas_call | solution.py:477
  37.8 0.8 %write.1 = (f32[1,256,128]{2,1,0:T(8,128)}, f32[2,256,128]{2,1,0:T(8,128)}) custom-call(f32[1,256,128]{2,1,0:T(8,128)S(1)} %get-tuple-element.4.bsol, f32[2,256,128]{2,1,0:T(8,128)S(1)} %get-tuple-element.5.tsol), custom_call_target="tpu_custom_call" | custom-call | tf_op jit(solution)/shard_map/write/pallas_call | solution.py:524
